TPU v7x, 128 devices: a whole 4x4x4 slice. The times are simulated.
128 devices in a mesh: tm: 32 (over z, y, x_lo), slab: 4 (over x_hi, core).
Axes of the slice: x: 4 (x_hi: 2, x_lo: 2; x = x_hi * 2 + x_lo), y: 4, z: 4, core: 2. Of those that a mesh axis runs over, the one named last changes fastest.
Arguments:
- kspace: bfloat16 [2, 64, 4, 96, 9984], P(None, 'tm', None, 'slab'), may hold values from -40 to 40, as said below
- sens: float32 [2, 4, 8, 104, 96], P(None, None, None, 'slab'), may hold values from -3 to 3
Outputs:
- projected: float32 [64, 2, 8, 104, 96], P('tm', None, None, 'slab')
Inputs may be any that keep to these rules, and one draw needn't show every extreme that they name: `kspace`: k-space values of order one with frames of different scale.
All inputs are finite; a program needn't handle non-finite values.
Results may differ from a plain program's by a relative error of at most 0.0036.
Values may be sent and summed in bfloat16 or wider, within the bound.
A program may use at most 128 MiB of HBM per device.

v0:
```python
import jax
import jax.numpy as jnp
from jax import lax
from jax.sharding import PartitionSpec as P

NX = 96
NY = 104
NZ = 96
RANK = 32
ITERS = 4
XW = 8


def inverse_table(length, count, offset):
    outputs = jnp.arange(count, dtype=jnp.int32) + offset
    inputs = jnp.arange(length, dtype=jnp.int32)
    phase = outputs[:, None] * inputs[None, :] % length
    angle = phase.astype(jnp.float32) * (2.0 * jnp.pi / length)
    norm_factor = 1.0 / jnp.sqrt(jnp.float32(length))
    return (jnp.cos(angle) * norm_factor, jnp.sin(angle) * norm_factor)


def contract(pattern, matrix_table, operand):
    return jnp.einsum(pattern, matrix_table, operand, precision=lax.Precision.HIGHEST)


def matmul(left, right):
    return jnp.dot(left, right, precision=lax.Precision.HIGHEST)


def orthonormal(rows, gram):
    factor = jnp.linalg.cholesky(matmul(matmul(rows, gram), rows.T))
    return lax.linalg.triangular_solve(factor, rows, left_side=True, lower=True)


def local(kspace, sens):
    frames_dev = kspace.shape[1]
    coil_count = kspace.shape[2]
    depth_dev = kspace.shape[3]
    spectrum = kspace.astype(jnp.float32).reshape(2, frames_dev, coil_count, depth_dev, NX, NY)
    across_cos, across_sin = inverse_table(NX, XW, (NX - XW) // 2)
    down_cos, down_sin = inverse_table(NY, NY, 0)
    depth_cos, depth_sin = inverse_table(NZ, NZ, 0)
    across_real = contract("jx,fczxy->fczjy", across_cos, spectrum[0]) - contract(
        "jx,fczxy->fczjy", across_sin, spectrum[1]
    )
    across_other = contract("jx,fczxy->fczjy", across_cos, spectrum[1]) + contract(
        "jx,fczxy->fczjy", across_sin, spectrum[0]
    )
    down_real = contract("my,fczjy->fczjm", down_cos, across_real) - contract(
        "my,fczjy->fczjm", down_sin, across_other
    )
    down_other = contract("my,fczjy->fczjm", down_cos, across_other) + contract(
        "my,fczjy->fczjm", down_sin, across_real
    )
    planes = jnp.stack([down_real, down_other]).astype(jnp.bfloat16)
    arrived = lax.all_to_all(planes, "slab", split_axis=5, concat_axis=3, tiled=True).astype(
        jnp.float32
    )
    depth_real = contract("wz,fczxy->fcxyw", depth_cos, arrived[0]) - contract(
        "wz,fczxy->fcxyw", depth_sin, arrived[1]
    )
    depth_other = contract("wz,fczxy->fcxyw", depth_cos, arrived[1]) + contract(
        "wz,fczxy->fcxyw", depth_sin, arrived[0]
    )
    sens_real = sens[0][None]
    sens_other = sens[1][None]
    combined_real = jnp.sum(sens_real * depth_real + sens_other * depth_other, axis=1)
    combined_other = jnp.sum(sens_real * depth_other - sens_other * depth_real, axis=1)
    matrix = jnp.stack([combined_real, combined_other], axis=1).reshape(frames_dev, -1)
    rows = lax.all_to_all(matrix, "tm", split_axis=1, concat_axis=0, tiled=True)
    gram = lax.psum(matmul(rows, rows.T), ("tm", "slab"))
    eye = jnp.eye(RANK, dtype=jnp.float32)
    current = jnp.concatenate([eye, eye], axis=1)
    for sweep_index in range(ITERS):
        current = matmul(orthonormal(current, gram), gram)
    coeff = orthonormal(current, gram)
    mixing = matmul(matmul(coeff, gram).T, coeff)
    projected = matmul(mixing, rows)
    projected = lax.all_to_all(projected, "tm", split_axis=0, concat_axis=1, tiled=True)
    return projected.reshape(frames_dev, 2, XW, -1, NZ)


def solution(mesh):
    in_specs = (P(None, "tm", None, "slab", None), P(None, None, None, "slab", None))
    out_specs = P("tm", None, None, "slab", None)
    return jax.shard_map(local, mesh=mesh, in_specs=in_specs, out_specs=out_specs, check_vma=False)
```

profile of v0, /device:TPU:0, one launch (start us, length us, event | category | flops | bytes accessed | tf_op | source)
XLA Modules:
  0.0 234.5 jit_solution(5598859404871233806)
XLA Ops:
  0.0 5.4 %fusion.180 = (bf16[1,2,4,24,9984]{4,3,2,1,0:T(8,128)(2,1)}, bf16[1,2,4,24,9984]{4,3,2,1,0:T(8,128)(2,1)}) fusion(bf16[2,2,4,24,9984]{4,3,2,1,0:T(8,128)(2,1)} %param.5), kind=kLoop, calls=%fused_computation.213 | loop fusion | bytes 15335424 | tf_op jit(solution)/shard_map/slice | solution.py:44
  5.4 13.7 %squeeze.16 = bf16[2,4,24,96,104]{4,3,2,1,0:T(8,128)(2,1)} reshape(bf16[1,2,4,24,9984]{4,3,2,1,0:T(8,128)(2,1)} %get-tuple-element.9) | data formatting | bytes 7667712 | tf_op jit(solution)/shard_map/squeeze | solution.py:44
  19.2 13.8 %squeeze.17 = bf16[2,4,24,96,104]{4,3,2,1,0:T(8,128)(2,1)} reshape(bf16[1,2,4,24,9984]{4,3,2,1,0:T(8,128)(2,1)} %get-tuple-element.10) | data formatting | bytes 7667712 | tf_op jit(solution)/shard_map/squeeze | solution.py:45
  33.0 4.3 %fusion.105 = f32[8,2,4,24,104]{4,0,3,2,1:T(8,128)S(1)} fusion(bf16[2,4,24,96,104]{4,3,2,1,0:T(8,128)(2,1)} %squeeze.16, s32[8]{0:T(128)S(1)} %iota_add_fusion), kind=kOutput, calls=%fused_computation.133 | convolution fusion | flops 184032768 | bytes 4472864 | tf_op jit(solution)/shard_map/jx,fczxy->fczjy/dot_general | solution.py:24
  37.3 2.1 fusion.103
  39.4 2.1 fusion.1
  41.4 1.0 fusion.10
  42.5 2.1 fusion
  44.5 1.0 fusion.6
  45.5 1.0 fusion.5
  46.5 1.0 fusion.4
  47.5 1.1 pad_maximum_fusion
  48.6 5.8 %copy.42 = bf16[2,2,4,24,8,104]{3,4,2,1,0,5:T(8,128)(2,1)S(1)} copy(bf16[2,2,4,24,8,104]{5,3,4,2,1,0:T(8,128)(2,1)} %pad_maximum_fusion) | data formatting | bytes 1277952 | tf_op jit(solution)/shard_map/stack | solution.py:56
  54.4 5.0 %reshape.64 = bf16[4,2,39936]{2,1,0:T(2,128)(2,1)} reshape(bf16[104,2,2,4,8,24]{5,4,3,2,1,0:T(8,128)(2,1)S(1)} %bitcast.164) | data formatting | bytes 1277952
  59.4 4.4 %all-to-all-start = ((bf16[4,2,39936]{2,1,0:T(2,128)(2,1)}), bf16[4,2,39936]{2,1,0:T(2,128)(2,1)}, u32[]{:S(2)}, u32[]{:S(2)}) async-start(bf16[4,2,39936]{2,1,0:T(2,128)(2,1)} %reshape.64), calls=%async_computation | async-start | bytes 1277952 | tf_op jit(solution)/shard_map/all_to_all | solution.py:57
  63.8 1.2 slice_bitcast_fusion.1
  65.0 0.9 copy.37
  65.9 0.9 copy.46
  66.8 8.7 %all-to-all-done = bf16[4,2,39936]{2,1,0:T(2,128)(2,1)} async-done(((bf16[4,2,39936]{2,1,0:T(2,128)(2,1)}), bf16[4,2,39936]{2,1,0:T(2,128)(2,1)}, u32[]{:S(2)}, u32[]{:S(2)}) %all-to-all-start) | async-done | bytes 639008 | tf_op jit(solution)/shard_map/all_to_all | solution.py:57
  75.5 5.6 %reshape.65 = bf16[104,2,2,4,8,24]{5,4,3,2,1,0:T(8,128)(2,1)S(1)} reshape(bf16[4,2,39936]{2,1,0:T(2,128)(2,1)} %all-to-all-done) | data formatting | bytes 1277952
  81.1 4.4 %copy.86 = bf16[2,2,4,24,8,4,26]{3,5,4,6,2,1,0:T(4,128)(2,1)S(1)} copy(bf16[2,2,4,24,8,4,26]{3,4,2,1,0,6,5:T(8,128)(2,1)S(1)} %bitcast.165) | data formatting | bytes 1277952 | tf_op jit(solution)/shard_map/all_to_all | solution.py:57
  85.5 1.2 fusion.181
  86.7 1.6 squeeze.18
  88.3 2.9 %fusion.16 = f32[2,4,8,26,96]{4,3,2,1,0:T(8,128)} fusion(bf16[2,4,96,8,26]{2,3,4,1,0:T(8,128)(2,1)} %squeeze.18), kind=kOutput, calls=%fused_computation.27 | convolution fusion | flops 184117248 | bytes 958464 | tf_op jit(solution)/shard_map/wz,fczxy->fcxyw/dot_general | solution.py:24
  91.1 0.9 squeeze.19
  92.0 0.8 fusion.12
  92.8 2.0 convolution_subtract_fusion
  94.9 2.2 add_reduce_fusion
  97.3 1.0 copy.49
  98.3 9.4 %all-to-all-start.1 = ((f32[2,32,1248]{2,0,1:T(2,128)}), f32[2,32,1248]{2,0,1:T(2,128)S(1)}, u32[]{:S(2)}, u32[]{:S(2)}) async-start(f32[2,32,1248]{2,0,1:T(2,128)} %copy.49), calls=%async_computation.1 | async-start | bytes 655360 | tf_op jit(solution)/shard_map/all_to_all | solution.py:71
  107.7 9.6 %all-to-all-done.1 = f32[2,32,1248]{2,0,1:T(2,128)S(1)} async-done(((f32[2,32,1248]{2,0,1:T(2,128)}), f32[2,32,1248]{2,0,1:T(2,128)S(1)}, u32[]{:S(2)}, u32[]{:S(2)}) %all-to-all-start.1) | async-done | bytes 319520 | tf_op jit(solution)/shard_map/all_to_all | solution.py:71
  118.2 62.4 %psum.7 = f32[64,64]{1,0:T(8,128)S(1)} all-reduce(f32[64,64]{1,0:T(8,128)S(1)} %fusion.182), channel_id=1, replica_groups=mesh['tm'=32,'slab'=4] {'tm','slab'}, use_global_device_ids=true, to_apply=%region_2.3 | all-reduce | flops 4096 | bytes 32768 | tf_op jit(solution)/shard_map/psum | solution.py:72
  181.1 2.9 %cholesky.89 = f32[32,32]{1,0:T(8,128)S(1)} custom-call(f32[32,32]{1,0:T(8,128)S(1)} %fusion.89), custom_call_target="Cholesky" | custom-call | tf_op jit(solution)/shard_map/jit(cholesky)/cholesky | solution.py:32
  184.7 0.7 fusion.70
  185.4 2.4 %custom-call.9 = f32[1,32,32]{1,2,0:T(8,128)S(1)} custom-call(f32[1,32,32]{2,1,0:T(8,128)S(1)} %fusion.70), custom_call_target="InvertDiagBlocksLowerTriangular" | custom-call | tf_op jit(solution)/shard_map/triangular_solve/custom-call.0 | solution.py:33
  188.6 2.9 %cholesky.100 = f32[32,32]{1,0:T(8,128)S(1)} custom-call(f32[32,32]{1,0:T(8,128)S(1)} %fusion.86), custom_call_target="Cholesky" | custom-call | tf_op jit(solution)/shard_map/jit(cholesky)/cholesky | solution.py:32
  192.2 0.7 fusion.71
  192.9 2.4 %custom-call.10 = f32[1,32,32]{1,2,0:T(8,128)S(1)} custom-call(f32[1,32,32]{2,1,0:T(8,128)S(1)} %fusion.71), custom_call_target="InvertDiagBlocksLowerTriangular" | custom-call | tf_op jit(solution)/shard_map/triangular_solve/custom-call.0 | solution.py:33
  196.1 2.9 %cholesky.111 = f32[32,32]{1,0:T(8,128)S(1)} custom-call(f32[32,32]{1,0:T(8,128)S(1)} %fusion.83), custom_call_target="Cholesky" | custom-call | tf_op jit(solution)/shard_map/jit(cholesky)/cholesky | solution.py:32
  199.7 0.7 fusion.72
  200.4 2.4 %custom-call.11 = f32[1,32,32]{1,2,0:T(8,128)S(1)} custom-call(f32[1,32,32]{2,1,0:T(8,128)S(1)} %fusion.72), custom_call_target="InvertDiagBlocksLowerTriangular" | custom-call | tf_op jit(solution)/shard_map/triangular_solve/custom-call.0 | solution.py:33
  203.6 2.9 %cholesky.122 = f32[32,32]{1,0:T(8,128)S(1)} custom-call(f32[32,32]{1,0:T(8,128)S(1)} %fusion.80), custom_call_target="Cholesky" | custom-call | tf_op jit(solution)/shard_map/jit(cholesky)/cholesky | solution.py:32
  207.2 0.7 fusion.73
  207.8 2.4 %custom-call.12 = f32[1,32,32]{1,2,0:T(8,128)S(1)} custom-call(f32[1,32,32]{2,1,0:T(8,128)S(1)} %fusion.73), custom_call_target="InvertDiagBlocksLowerTriangular" | custom-call | tf_op jit(solution)/shard_map/triangular_solve/custom-call.0 | solution.py:33
  211.1 2.9 %cholesky.133 = f32[32,32]{1,0:T(8,128)S(1)} custom-call(f32[32,32]{1,0:T(8,128)S(1)} %fusion.77), custom_call_target="Cholesky" | custom-call | tf_op jit(solution)/shard_map/jit(cholesky)/cholesky | solution.py:32
  215.3 2.4 %custom-call.13 = f32[1,32,32]{1,2,0:T(8,128)S(1)} custom-call(f32[1,32,32]{2,1,0:T(8,128)S(1)} %fusion.74), custom_call_target="InvertDiagBlocksLowerTriangular" | custom-call | tf_op jit(solution)/shard_map/triangular_solve/custom-call.0 | solution.py:33
  219.1 14.0 %all_to_all.47 = f32[32,2,1248]{2,1,0:T(2,128)S(1)} all-to-all(f32[32,2,1248]{2,1,0:T(2,128)S(1)} %copy.56), channel_id=1, replica_groups=mesh['tm'=32,'slab'=4] {'tm'}, dimensions={0} | all-to-all | bytes 638976 | tf_op jit(solution)/shard_map/all_to_all | solution.py:80
  233.4 1.0 copy.58
  (64 shorter events, 10.3 us)
Async XLA Ops:
  33.0 4.3 %copy-start = (bf16[2,4,24,96,104]{4,3,2,1,0:T(8,128)(2,1)S(1)}, bf16[2,4,24,96,104]{4,3,2,1,0:T(8,128)(2,1)}, u32[]{:S(2)}) copy-start(bf16[2,4,24,96,104]{4,3,2,1,0:T(8,128)(2,1)} %squeeze.17) | copy-start | bytes 11501572
  37.3 5.1 %slice-start = ((s8[4718592]{0:T(1024)(128)(4,1)}), s8[4194304]{0:T(1024)(128)(4,1)S(1)}, s32[]{:S(2)}) async-start(s8[4718592]{0:T(1024)(128)(4,1)} %bitcast.161), calls=%async_computation.3 | async-start | bytes 8388608
  39.4 3.1 %slice-start.1 = ((s8[4718592]{0:T(1024)(128)(4,1)}), s8[524288]{0:T(1024)(128)(4,1)S(1)}, s32[]{:S(2)}) async-start(s8[4718592]{0:T(1024)(128)(4,1)} %bitcast.161), calls=%async_computation.4 | async-start | bytes 1048576
  59.4 16.1 %all-to-all-start = ((bf16[4,2,39936]{2,1,0:T(2,128)(2,1)}), bf16[4,2,39936]{2,1,0:T(2,128)(2,1)}, u32[]{:S(2)}, u32[]{:S(2)}) async-start(bf16[4,2,39936]{2,1,0:T(2,128)(2,1)} %reshape.64), calls=%async_computation | async-start | bytes 1277952 | tf_op jit(solution)/shard_map/all_to_all | solution.py:57
  88.3 6.6 %copy-start.1 = (bf16[2,4,96,8,26]{2,3,4,1,0:T(8,128)(2,1)S(1)}, bf16[2,4,96,8,26]{2,3,4,1,0:T(8,128)(2,1)}, u32[]{:S(2)}) copy-start(bf16[2,4,96,8,26]{2,3,4,1,0:T(8,128)(2,1)} %squeeze.18) | copy-start | bytes 958468
  88.3 6.6 %copy-start.2 = (f32[4,8,26,96]{3,2,1,0:T(8,128)S(1)}, f32[4,8,26,96]{3,2,1,0:T(8,128)}, u32[]{:S(2)}) copy-start(f32[4,8,26,96]{3,2,1,0:T(8,128)} %copy.37) | copy-start | bytes 958468
  98.3 19.0 %all-to-all-start.1 = ((f32[2,32,1248]{2,0,1:T(2,128)}), f32[2,32,1248]{2,0,1:T(2,128)S(1)}, u32[]{:S(2)}, u32[]{:S(2)}) async-start(f32[2,32,1248]{2,0,1:T(2,128)} %copy.49), calls=%async_computation.1 | async-start | bytes 655360 | tf_op jit(solution)/shard_map/all_to_all | solution.py:71
where the time goes:
time: 235 us; the launch traced here: 234 us
  blocking collectives  76.4 us (33%)
  local copies, waits for them, and re-layouts  64.1 us (27%)
  other arithmetic  34.6 us (15%)
  matrix products  26.8 us (11%)
  waiting for transfers between devices  18.3 us (8%)
  starting transfers between devices  13.7 us (6%)
    psum x1, blocking collectives, local(): gram = lax.psum(matmul(rows, rows.T), ('tm', 'slab'))  62.4 us
    dot_general x12, matrix products, contract(): jnp.einsum(pattern, matrix_table, operand, precision=lax.Precision.HIGHEST)  22.3 us
    another operation x16, other arithmetic, orthonormal(): factor = jnp.linalg.cholesky(matmul(matmul(rows, gram), rows.T))  18 us
    another operation x10, other arithmetic, orthonormal(): return lax.linalg.triangular_solve(factor, rows, left_side=True, lower=True)  15.4 us
    all_to_all x1, blocking collectives, local(): lax.all_to_all(projected, 'tm', split_axis=0, concat_axis=1, tiled=True)  14 us
    squeeze x1, local copies, waits for them, and re-layouts, local(): spectrum[1]  13.8 us
    squeeze x1, local copies, waits for them, and re-layouts, local(): spectrum[0]  13.7 us
    unnamed x12, local copies, waits for them, and re-layouts  10.6 us
  transfers between devices with their start and end apart: 2, of which 2 were waited for; matrix products, arithmetic and copies ran while one was open for 1% of the time, Pallas kernels for 0%

commit v1 on v0

--- a/solution.py
+++ b/solution.py
@@ -69,7 +69,9 @@
     combined_other = jnp.sum(sens_real * depth_other - sens_other * depth_real, axis=1)
     matrix = jnp.stack([combined_real, combined_other], axis=1).reshape(frames_dev, -1)
     rows = lax.all_to_all(matrix, "tm", split_axis=1, concat_axis=0, tiled=True)
-    gram = lax.psum(matmul(rows, rows.T), ("tm", "slab"))
+    x = matmul(rows, rows.T)
+    parts = lax.all_gather(x, ("tm", "slab"))
+    gram = jnp.sum(parts, axis=0)
     eye = jnp.eye(RANK, dtype=jnp.float32)
     current = jnp.concatenate([eye, eye], axis=1)
     for sweep_index in range(ITERS):

time: 235 us -> 383 us (1.63)
  waiting for transfers between devices: 18.3 us -> 203 us
  blocking collectives: 76.4 us -> 34.1 us
  between operations: 0.48 us -> 13.9 us
  starting transfers between devices: 13.7 us -> 4.38 us
    all_gather x0 -> x1, waiting for transfers between devices: none -> 194 us  [local(): parts = lax.all_gather(x, ('tm', 'slab'))]
    psum x1 -> x0, blocking collectives: 62.4 us -> none  [local(): gram = lax.psum(matmul(rows, rows.T), ('tm', 'slab'))]
    all_to_all x0 -> x1, blocking collectives: none -> 18.8 us  [local(): rows = lax.all_to_all(matrix, 'tm', split_axis=1, concat_axis=0, tiled=True)]
    all_to_all x1 -> x0, waiting for transfers between devices: 9.63 us -> none  [local(): rows = lax.all_to_all(matrix, 'tm', split_axis=1, concat_axis=0, tiled=True)]
    all_to_all x1 -> x0, starting transfers between devices: 9.35 us -> none  [local(): rows = lax.all_to_all(matrix, 'tm', split_axis=1, concat_axis=0, tiled=True)]
where the time goes in v1:
time: 383 us
  waiting for transfers between devices  203 us (53%)
  local copies, waits for them, and re-layouts  63.4 us (17%)
  other arithmetic  37.1 us (10%)
  blocking collectives  34.1 us (9%)
  matrix products  27.4 us (7%)
  between operations  13.9 us (4%)
  starting transfers between devices  4.38 us (1%)
    all_gather x1, waiting for transfers between devices, local(): parts = lax.all_gather(x, ('tm', 'slab'))  194 us
    dot_general x12, matrix products, contract(): jnp.einsum(pattern, matrix_table, operand, precision=lax.Precision.HIGHEST)  22.3 us
    all_to_all x1, blocking collectives, local(): rows = lax.all_to_all(matrix, 'tm', split_axis=1, concat_axis=0, tiled=True)  18.8 us
    another operation x16, other arithmetic, orthonormal(): factor = jnp.linalg.cholesky(matmul(matmul(rows, gram), rows.T))  18 us
    another operation x10, other arithmetic, orthonormal(): return lax.linalg.triangular_solve(factor, rows, left_side=True, lower=True)  15.4 us
    all_to_all x1, blocking collectives, local(): lax.all_to_all(projected, 'tm', split_axis=0, concat_axis=1, tiled=True)  15.2 us
    squeeze x1, local copies, waits for them, and re-layouts, local(): spectrum[1]  13.8 us
    squeeze x1, local copies, waits for them, and re-layouts, local(): spectrum[0]  13.7 us
  transfers between devices with their start and end apart: 2, of which 2 were waited for; matrix products, arithmetic and copies ran while one was open for 1% of the time, Pallas kernels for 0%

profile of v1, /device:TPU:0, one launch (start us, length us, event | category | flops | bytes accessed | tf_op | source)
XLA Modules:
  0.0 382.8 jit_solution(10691633709992010446)
XLA Ops:
  6.5 5.4 %fusion.180 = (bf16[1,2,4,24,9984]{4,3,2,1,0:T(8,128)(2,1)}, bf16[1,2,4,24,9984]{4,3,2,1,0:T(8,128)(2,1)}) fusion(bf16[2,2,4,24,9984]{4,3,2,1,0:T(8,128)(2,1)} %param.5), kind=kLoop, calls=%fused_computation.213 | loop fusion | bytes 15335424 | tf_op jit(solution)/shard_map/slice | solution.py:44
  12.0 13.7 %squeeze.16 = bf16[2,4,24,96,104]{4,3,2,1,0:T(8,128)(2,1)} reshape(bf16[1,2,4,24,9984]{4,3,2,1,0:T(8,128)(2,1)} %get-tuple-element.9) | data formatting | bytes 7667712 | tf_op jit(solution)/shard_map/squeeze | solution.py:44
  25.7 13.8 %squeeze.17 = bf16[2,4,24,96,104]{4,3,2,1,0:T(8,128)(2,1)} reshape(bf16[1,2,4,24,9984]{4,3,2,1,0:T(8,128)(2,1)} %get-tuple-element.10) | data formatting | bytes 7667712 | tf_op jit(solution)/shard_map/squeeze | solution.py:45
  39.6 4.3 %fusion.105 = f32[8,2,4,24,104]{4,0,3,2,1:T(8,128)S(1)} fusion(bf16[2,4,24,96,104]{4,3,2,1,0:T(8,128)(2,1)} %squeeze.16, s32[8]{0:T(128)S(1)} %iota_add_fusion), kind=kOutput, calls=%fused_computation.133 | convolution fusion | flops 184032768 | bytes 4472864 | tf_op jit(solution)/shard_map/jx,fczxy->fczjy/dot_general | solution.py:24
  43.9 2.1 fusion.103
  45.9 2.1 fusion.1
  48.0 1.0 fusion.10
  49.0 2.1 fusion
  51.1 1.0 fusion.6
  52.1 1.0 fusion.5
  53.1 1.0 fusion.4
  54.1 1.1 pad_maximum_fusion
  55.1 5.8 %copy.42 = bf16[2,2,4,24,8,104]{3,4,2,1,0,5:T(8,128)(2,1)S(1)} copy(bf16[2,2,4,24,8,104]{5,3,4,2,1,0:T(8,128)(2,1)} %pad_maximum_fusion) | data formatting | bytes 1277952 | tf_op jit(solution)/shard_map/stack | solution.py:56
  60.9 5.0 %reshape.65 = bf16[4,2,39936]{2,1,0:T(2,128)(2,1)} reshape(bf16[104,2,2,4,8,24]{5,4,3,2,1,0:T(8,128)(2,1)S(1)} %bitcast.165) | data formatting | bytes 1277952
  65.9 4.4 %all-to-all-start = ((bf16[4,2,39936]{2,1,0:T(2,128)(2,1)}), bf16[4,2,39936]{2,1,0:T(2,128)(2,1)}, u32[]{:S(2)}, u32[]{:S(2)}) async-start(bf16[4,2,39936]{2,1,0:T(2,128)(2,1)} %reshape.65), calls=%async_computation | async-start | bytes 1277952 | tf_op jit(solution)/shard_map/all_to_all | solution.py:57
  70.3 1.2 slice_bitcast_fusion.1
  71.5 0.9 copy.37
  72.4 0.9 copy.46
  73.3 8.7 %all-to-all-done = bf16[4,2,39936]{2,1,0:T(2,128)(2,1)} async-done(((bf16[4,2,39936]{2,1,0:T(2,128)(2,1)}), bf16[4,2,39936]{2,1,0:T(2,128)(2,1)}, u32[]{:S(2)}, u32[]{:S(2)}) %all-to-all-start) | async-done | bytes 639008 | tf_op jit(solution)/shard_map/all_to_all | solution.py:57
  82.0 5.6 %reshape.66 = bf16[104,2,2,4,8,24]{5,4,3,2,1,0:T(8,128)(2,1)S(1)} reshape(bf16[4,2,39936]{2,1,0:T(2,128)(2,1)} %all-to-all-done) | data formatting | bytes 1277952
  87.6 4.4 %copy.86 = bf16[2,2,4,24,8,4,26]{3,5,4,6,2,1,0:T(4,128)(2,1)S(1)} copy(bf16[2,2,4,24,8,4,26]{3,4,2,1,0,6,5:T(8,128)(2,1)S(1)} %bitcast.166) | data formatting | bytes 1277952 | tf_op jit(solution)/shard_map/all_to_all | solution.py:57
  92.0 1.2 fusion.181
  93.2 1.6 squeeze.18
  94.8 2.9 fusion.16
  97.7 0.9 squeeze.19
  98.6 0.8 fusion.12
  99.3 2.0 convolution_subtract_fusion
  101.4 2.2 add_reduce_fusion
  104.1 18.8 %all_to_all.47 = f32[2,32,1248]{2,0,1:T(2,128)S(1)} all-to-all(f32[2,32,1248]{2,0,1:T(2,128)S(1)} %copy.49), channel_id=1, replica_groups=mesh['tm'=32,'slab'=4] {'tm'}, dimensions={1} | all-to-all | bytes 638976 | tf_op jit(solution)/shard_map/all_to_all | solution.py:71
  123.1 1.0 fusion.182
  124.4 193.9 %all-gather.3.cloned.1.call-done = f32[8192,64]{1,0:T(8,128)} async-done(((f32[64,64]{1,0:T(8,128)}), f32[8192,64]{1,0:T(8,128)}) %all-gather.3.cloned.1.call-update) | async-done | bytes 2097168 | tf_op jit(solution)/shard_map/all_gather | solution.py:73
  318.3 2.5 reduce_sum.29
  321.3 2.9 cholesky.89
  324.9 0.7 fusion.70
  325.6 2.4 custom-call.9
  328.8 2.9 cholesky.100
  332.4 0.7 fusion.71
  333.1 2.4 custom-call.10
  336.3 2.9 cholesky.111
  339.9 0.7 fusion.72
  340.6 2.4 custom-call.11
  343.8 2.9 cholesky.122
  347.4 0.7 fusion.73
  348.1 2.4 custom-call.12
  351.3 2.9 cholesky.133
  355.6 2.4 custom-call.13
  359.3 15.2 %all_to_all.48 = f32[32,2,1248]{2,1,0:T(2,128)S(1)} all-to-all(f32[32,2,1248]{2,1,0:T(2,128)S(1)} %copy.56), channel_id=1, replica_groups=mesh['tm'=32,'slab'=4] {'tm'}, dimensions={0} | all-to-all | bytes 638976 | tf_op jit(solution)/shard_map/all_to_all | solution.py:82
  374.9 1.0 copy.58
  (66 shorter events, 10.2 us)
Async XLA Ops:
  39.6 4.3 %copy-start = (bf16[2,4,24,96,104]{4,3,2,1,0:T(8,128)(2,1)S(1)}, bf16[2,4,24,96,104]{4,3,2,1,0:T(8,128)(2,1)}, u32[]{:S(2)}) copy-start(bf16[2,4,24,96,104]{4,3,2,1,0:T(8,128)(2,1)} %squeeze.17) | copy-start | bytes 11501572
  43.8 5.1 %slice-start = ((s8[4718592]{0:T(1024)(128)(4,1)}), s8[4194304]{0:T(1024)(128)(4,1)S(1)}, s32[]{:S(2)}) async-start(s8[4718592]{0:T(1024)(128)(4,1)} %bitcast.162), calls=%async_computation.4 | async-start | bytes 8388608
  45.9 3.1 slice-start.1
  65.9 16.1 %all-to-all-start = ((bf16[4,2,39936]{2,1,0:T(2,128)(2,1)}), bf16[4,2,39936]{2,1,0:T(2,128)(2,1)}, u32[]{:S(2)}, u32[]{:S(2)}) async-start(bf16[4,2,39936]{2,1,0:T(2,128)(2,1)} %reshape.65), calls=%async_computation | async-start | bytes 1277952 | tf_op jit(solution)/shard_map/all_to_all | solution.py:57
  70.3 248.0 %all-gather.3.cloned.1.call-start = ((), (), s32[]{:S(2)}) async-start(), calls=%async_computation.3 | async-start | bytes 4227072 | tf_op jit(solution)/shard_map/all_gather | solution.py:73
  94.8 6.6 %copy-start.1 = (bf16[2,4,96,8,26]{2,3,4,1,0:T(8,128)(2,1)S(1)}, bf16[2,4,96,8,26]{2,3,4,1,0:T(8,128)(2,1)}, u32[]{:S(2)}) copy-start(bf16[2,4,96,8,26]{2,3,4,1,0:T(8,128)(2,1)} %squeeze.18) | copy-start | bytes 958468
  94.8 6.6 %copy-start.2 = (f32[4,8,26,96]{3,2,1,0:T(8,128)S(1)}, f32[4,8,26,96]{3,2,1,0:T(8,128)}, u32[]{:S(2)}) copy-start(f32[4,8,26,96]{3,2,1,0:T(8,128)} %copy.37) | copy-start | bytes 958468
Sparse Core Ops, SparseCore 0:
  124.3 193.9 all-gather.2
